TPU v7x, 32 devices: a whole 2x2x4 slice. The times are simulated.
32 devices in a mesh: dp: 4 (over y, x), expert: 8 (over z, core).
Axes of the slice: x: 2, y: 2, z: 4, core: 2. Of those that a mesh axis runs over, the one named last changes fastest.
Arguments:
- tokens: bfloat16 [1024, 2048], P(('dp', 'expert')), may hold values from -6 to 6
- tangent: bfloat16 [1024, 2048], P(('dp', 'expert')), may hold values from -6 to 6
- norm_gain: float32 [2048], replicated, may hold values from 0.1 to 1.9
- router: bfloat16 [2048, 16], replicated, may hold values from -0.125 to 0.125
- w_gate: bfloat16 [16, 2048, 768], P('expert', 'dp'), may hold values from -0.125 to 0.125
- w_up: bfloat16 [16, 2048, 768], P('expert', 'dp'), may hold values from -0.125 to 0.125
- w_down: bfloat16 [16, 768, 2048], P('expert', None, 'dp'), may hold values from -0.21875 to 0.21875
- routes: int32 [1024, 8], P(('dp', 'expert')), may hold values from 0 to 15, all different within a row; in each aligned block of 32 rows (0 to 31, 32 to 63, ...) at most 32 rows name the same one
Outputs:
- tangent_image: float32 [1024, 2048], P(('dp', 'expert'))
- gram_image: float32 [1024, 2048], P(('dp', 'expert'))
Inputs may be any that keep to these rules, and one draw needn't show every extreme that they name: `routes`: each row names 8 different experts. Within the rows of one device (aligned blocks of 32 rows) no expert is named more than 32 times, and in some such blocks an expert is named exactly 32 times.
All inputs are finite; a program needn't handle non-finite values.
Results may differ from a plain program's by a relative error of at most 0.013.
Values may be sent and summed in bfloat16 or wider, within the bound.
A program may use at most 128 MiB of HBM per device.

v0:
```python
import jax
import jax.numpy as jnp
from jax import lax
from jax.sharding import PartitionSpec as P

eps_value = 1e-06


def pick_columns(table, routes):
    hits = routes[:, :, None] == jnp.arange(table.shape[1], dtype=jnp.int32)[None, None, :]
    return jnp.sum(jnp.where(hits, table[:, None, :], jnp.zeros((), table.dtype)), axis=2)


def on_device(tokens, tangent, norm_gain, router, w_gate, w_up, w_down, routes):
    tok_rows, topk = routes.shape
    model_width = tokens.shape[1]
    experts_all = router.shape[1]
    local_experts = w_gate.shape[0]
    groups = lax.axis_size("expert")
    capacity = 2 * tok_rows * topk // experts_all
    xfull = tokens.astype(jnp.float32)
    vfull = tangent.astype(jnp.float32)
    inv_rms = lax.rsqrt(jnp.mean(xfull * xfull, axis=1, keepdims=True) + eps_value)
    normed = (norm_gain * xfull * inv_rms).astype(jnp.bfloat16)
    cross_term = jnp.mean(xfull * vfull, axis=1, keepdims=True)
    normed_tan = (norm_gain * (vfull * inv_rms - xfull * inv_rms**3 * cross_term)).astype(
        jnp.bfloat16
    )
    logits = jnp.dot(normed, router, preferred_element_type=jnp.float32)
    logit_tan = jnp.dot(normed_tan, router, preferred_element_type=jnp.float32)
    selected = pick_columns(logits, routes)
    sel_tan = pick_columns(logit_tan, routes)
    exp_sel = jnp.exp(selected)
    gate_prob = exp_sel / jnp.sum(exp_sel, axis=1, keepdims=True)
    gate_tan = gate_prob * (sel_tan - jnp.sum(gate_prob * sel_tan, axis=1, keepdims=True))
    gate_b = gate_prob.astype(jnp.bfloat16)
    gate_tan_b = gate_tan.astype(jnp.bfloat16)
    pair_count = tok_rows * topk
    flat_ids = routes.reshape(-1)
    onehot = (flat_ids[:, None] == jnp.arange(experts_all, dtype=jnp.int32)[None, :]).astype(
        jnp.int32
    )
    slot_rank = jnp.sum(onehot * jnp.cumsum(onehot, axis=0), axis=1) - 1
    slot_of_pair = flat_ids * capacity + slot_rank
    slot_table = jnp.full((experts_all * capacity,), -1, jnp.int32)
    slot_table = slot_table.at[slot_of_pair].set(jnp.arange(pair_count, dtype=jnp.int32))
    slot_valid = slot_table >= 0
    safe_pair = jnp.maximum(slot_table, 0)
    tok_idx = safe_pair // topk
    which_k = safe_pair % topk
    bf_zero = jnp.zeros((), jnp.bfloat16)
    send_rows = jnp.stack(
        (
            jnp.where(slot_valid[:, None], normed[tok_idx], bf_zero),
            jnp.where(slot_valid[:, None], normed_tan[tok_idx], bf_zero),
        )
    )
    send_rows = send_rows.reshape(2, groups, local_experts * capacity, model_width)
    send_gates = jnp.stack(
        (
            jnp.where(slot_valid, gate_b[tok_idx, which_k], bf_zero),
            jnp.where(slot_valid, gate_tan_b[tok_idx, which_k], bf_zero),
        )
    )
    send_gates = send_gates.reshape(2, groups, local_experts * capacity)
    recv_rows, recv_gates = (
        lax.all_to_all(send_rows, "expert", split_axis=1, concat_axis=1, tiled=True),
        lax.all_to_all(send_gates, "expert", split_axis=1, concat_axis=1, tiled=True),
    )
    slot_rows = recv_rows.reshape(2, groups, local_experts, capacity, model_width)
    recv_gates = recv_gates.reshape(2, groups, local_experts, capacity).astype(jnp.float32)
    gate_val = recv_gates[0][..., None]
    tan_val = recv_gates[1][..., None]
    gate_full, up_full, down_full = (
        lax.all_gather(w_gate, "dp", axis=1, tiled=True),
        lax.all_gather(w_up, "dp", axis=1, tiled=True),
        lax.all_gather(w_down, "dp", axis=2, tiled=True),
    )
    pre_both = jnp.einsum(
        "tslkd,ldf->tslkf", slot_rows, gate_full, preferred_element_type=jnp.float32
    )
    up_both = jnp.einsum("tslkd,ldf->tslkf", slot_rows, up_full, preferred_element_type=jnp.float32)
    pre_gate = pre_both[0]
    gate_dot = pre_both[1]
    pre_up = up_both[0]
    up_dot = up_both[1]
    sig_gate = jax.nn.sigmoid(pre_gate)
    silu_gate = pre_gate * sig_gate
    slope_gate = sig_gate * (1.0 + pre_gate * (1.0 - sig_gate))
    hidden = silu_gate * pre_up
    hidden_tan = slope_gate * gate_dot * pre_up + silu_gate * up_dot
    mixed_rows = (tan_val * hidden + gate_val * hidden_tan).astype(jnp.bfloat16)
    pair_image = jnp.einsum(
        "slkf,lfd->slkd", mixed_rows, down_full, preferred_element_type=jnp.float32
    )
    pair_send = pair_image.astype(jnp.bfloat16).reshape(
        groups, local_experts * capacity, model_width
    )
    pair_back = lax.all_to_all(pair_send, "expert", split_axis=0, concat_axis=0, tiled=True)
    pair_back = pair_back.reshape(experts_all * capacity, model_width)
    tangent_image = jnp.sum(
        pair_back[slot_of_pair].astype(jnp.float32).reshape(tok_rows, topk, model_width), axis=1
    )
    image_b = tangent_image.astype(jnp.bfloat16)
    send_cot = jnp.where(slot_valid[:, None], image_b[tok_idx], bf_zero).reshape(
        groups, local_experts * capacity, model_width
    )
    recv_cot = lax.all_to_all(send_cot, "expert", split_axis=0, concat_axis=0, tiled=True)
    recv_cot = recv_cot.reshape(groups, local_experts, capacity, model_width)
    back_hidden = jnp.einsum(
        "slkd,lfd->slkf", recv_cot, down_full, preferred_element_type=jnp.float32
    )
    gate_cot = jnp.sum(back_hidden * hidden, axis=3).astype(jnp.bfloat16)
    scaled = gate_val * back_hidden
    grad_gate = (scaled * pre_up * slope_gate).astype(jnp.bfloat16)
    grad_up = (scaled * silu_gate).astype(jnp.bfloat16)
    pair_grad = jnp.einsum(
        "slkf,ldf->slkd", grad_gate, gate_full, preferred_element_type=jnp.float32
    )
    pair_grad = pair_grad + jnp.einsum(
        "slkf,ldf->slkd", grad_up, up_full, preferred_element_type=jnp.float32
    )
    grad_send = pair_grad.astype(jnp.bfloat16).reshape(
        groups, local_experts * capacity, model_width
    )
    cot_send = gate_cot.reshape(groups, local_experts * capacity)
    grad_back, cot_back = (
        lax.all_to_all(grad_send, "expert", split_axis=0, concat_axis=0, tiled=True),
        lax.all_to_all(cot_send, "expert", split_axis=0, concat_axis=0, tiled=True),
    )
    grad_back = grad_back.reshape(experts_all * capacity, model_width)
    cot_back = cot_back.reshape(experts_all * capacity)
    expert_grad = jnp.sum(
        grad_back[slot_of_pair].astype(jnp.float32).reshape(tok_rows, topk, model_width), axis=1
    )
    pair_cot = cot_back[slot_of_pair].astype(jnp.float32).reshape(tok_rows, topk)
    logit_grad = gate_prob * (pair_cot - jnp.sum(gate_prob * pair_cot, axis=1, keepdims=True))
    hits = routes[:, :, None] == jnp.arange(experts_all, dtype=jnp.int32)[None, None, :]
    column_grad = jnp.sum(jnp.where(hits, logit_grad[:, :, None], 0.0), axis=1)
    router_grad = jnp.dot(
        column_grad, router.astype(jnp.float32).T, precision=lax.Precision.HIGHEST
    )
    pulled = norm_gain * (expert_grad + router_grad)
    gram_image = inv_rms * pulled - xfull * inv_rms**3 * jnp.mean(
        pulled * xfull, axis=1, keepdims=True
    )
    return (tangent_image, gram_image)


def solution(mesh):
    in_specs = (
        P(("dp", "expert"), None),
        P(("dp", "expert"), None),
        P(),
        P(),
        P("expert", "dp", None),
        P("expert", "dp", None),
        P("expert", None, "dp"),
        P(("dp", "expert"), None),
    )
    out_specs = (P(("dp", "expert"), None), P(("dp", "expert"), None))
    return jax.shard_map(
        on_device, mesh=mesh, in_specs=in_specs, out_specs=out_specs, check_vma=False
    )
```

profile of v0, /device:TPU:0, one launch (start us, length us, event | category | flops | bytes accessed | tf_op | source)
XLA Modules:
  0.0 431.5 jit_solution(7534912825999140683)
XLA Ops:
  10.1 1.4 scatter_custom_fusion
  12.3 4.6 %gather_fusion.1 = bf16[512]{0:T(512)(128)(2,1)S(1)} fusion(bf16[32,8]{0,1:T(8,128)(2,1)S(1)} %get-tuple-element.12, s32[512]{0:T(512)S(1)} %get-tuple-element.14), kind=kCustom, calls=%fused_computation.1 | custom fusion | bytes 6144 | tf_op jit(solution)/shard_map/gather | solution.py:62
  17.0 4.6 %gather_fusion = bf16[512]{0:T(512)(128)(2,1)S(1)} fusion(bf16[32,8]{0,1:T(8,128)(2,1)S(1)} %get-tuple-element.13, s32[512]{0:T(512)S(1)} %get-tuple-element.14), kind=kCustom, calls=%fused_computation | custom fusion | bytes 6144 | tf_op jit(solution)/shard_map/gather | solution.py:61
  22.4 6.3 %all-to-all-start = ((bf16[2,8,64]{2,0,1:T(2,128)(2,1)}), bf16[2,8,64]{2,0,1:T(2,128)(2,1)S(1)}, u32[]{:S(2)}, u32[]{:S(2)}) async-start(bf16[2,8,64]{2,0,1:T(2,128)(2,1)} %copy.122), calls=%async_computation | async-start | bytes 8192 | tf_op jit(solution)/shard_map/all_to_all | solution.py:68
  28.8 2.5 gather_fusion.3
  31.3 3.3 gather_fusion.2
  34.6 1.9 broadcast_select_fusion.2
  36.5 2.4 pad_maximum_fusion
  38.9 5.1 %all-to-all-start.1 = ((bf16[2,8,64,2048]{3,2,0,1:T(8,128)(2,1)}), bf16[2,8,64,2048]{3,2,0,1:T(8,128)(2,1)}, u32[]{:S(2)}, u32[]{:S(2)}) async-start(bf16[2,8,64,2048]{3,2,0,1:T(8,128)(2,1)} %pad_maximum_fusion), calls=%async_computation.1 | async-start | bytes 8388608 | tf_op jit(solution)/shard_map/all_to_all | solution.py:67
  44.9 93.2 %all-to-all-done.1 = bf16[2,8,64,2048]{3,2,0,1:T(8,128)(2,1)} async-done(((bf16[2,8,64,2048]{3,2,0,1:T(8,128)(2,1)}), bf16[2,8,64,2048]{3,2,0,1:T(8,128)(2,1)}, u32[]{:S(2)}, u32[]{:S(2)}) %all-to-all-start.1) | async-done | bytes 4194336 | tf_op jit(solution)/shard_map/all_to_all | solution.py:67
  138.1 9.1 %fusion.27 = f32[2,8,2,32,768]{4,3,1,0,2:T(8,128)} fusion(bf16[2,2048,768]{2,1,0:T(8,128)(2,1)} %all-gather.4.cloned.1.call-done, bf16[2,8,2,32,2048]{4,3,2,0,1:T(8,128)(2,1)} %bitcast.8), kind=kOutput, calls=%fused_computation.36 | convolution fusion | flops 3221225472 | bytes 13631488 | tf_op jit(solution)/shard_map/tslkd,ldf->tslkf/dot_general | solution.py:79
  147.2 7.6 %all-gather.6.cloned.1.call-done = bf16[2,2048,768]{2,1,0:T(8,128)(2,1)} async-done(((bf16[2,512,768]{2,1,0:T(8,128)(2,1)}), bf16[2,2048,768]{2,1,0:T(8,128)(2,1)}) %all-gather.6.cloned.1.call-update) | async-done | bytes 6291472 | tf_op jit(solution)/shard_map/all_gather | solution.py:76
  154.8 9.2 %fusion.32 = f32[2,8,2,32,768]{4,3,1,2,0:T(8,128)} fusion(bf16[2,2048,768]{2,1,0:T(8,128)(2,1)} %all-gather.6.cloned.1.call-done, bf16[2,8,2,32,2048]{4,3,2,0,1:T(8,128)(2,1)} %bitcast.8), kind=kOutput, calls=%fused_computation.37 | convolution fusion | flops 3221225472 | bytes 13631488 | tf_op jit(solution)/shard_map/tslkd,ldf->tslkf/dot_general | solution.py:82
  164.0 62.7 %all-gather.8.cloned.1.call-done = bf16[2,768,2048]{2,1,0:T(8,128)(2,1)} async-done(((bf16[2,768,512]{2,1,0:T(8,128)(2,1)}), bf16[2,768,2048]{2,1,0:T(8,128)(2,1)}) %all-gather.8.cloned.1.call-update) | async-done | bytes 6291472 | tf_op jit(solution)/shard_map/all_gather | solution.py:77
  226.7 7.2 %fusion.22 = bf16[8,2,32,2048]{3,2,0,1:T(8,128)(2,1)S(1)} fusion(bf16[2,768,2048]{2,1,0:T(8,128)(2,1)} %all-gather.8.cloned.1.call-done, f32[2,8,2,32,768]{4,3,1,2,0:T(8,128)} %fusion.32, f32[2,8,2,32,768]{4,3,1,0,2:T(8,128)} %fusion.27, f32[8,2,32]{2,0,1:T(8,128)S(1)} %copy.131, f32[8,2,32]{2,0,1:T(8,128)S(1)} %copy.123), kind=kOutput, calls=%fused_computation.27 | convolution fusion | flops 1618345984 | bytes 14684160 | tf_op jit(solution)/shard_map/slkf,lfd->slkd/dot_general | solution.py:93
  233.9 1.4 copy.132
  235.3 4.6 %all-to-all-start.2 = ((bf16[8,64,2048]{2,1,0:T(8,128)(2,1)}), bf16[8,64,2048]{2,1,0:T(8,128)(2,1)S(1)}, u32[]{:S(2)}, u32[]{:S(2)}) async-start(bf16[8,64,2048]{2,1,0:T(8,128)(2,1)} %bitcast.169), calls=%async_computation.2 | async-start | bytes 4194304 | tf_op jit(solution)/shard_map/all_to_all | solution.py:99
  239.9 49.1 %all-to-all-done.2 = bf16[8,64,2048]{2,1,0:T(8,128)(2,1)S(1)} async-done(((bf16[8,64,2048]{2,1,0:T(8,128)(2,1)}), bf16[8,64,2048]{2,1,0:T(8,128)(2,1)S(1)}, u32[]{:S(2)}, u32[]{:S(2)}) %all-to-all-start.2) | async-done | bytes 2097184 | tf_op jit(solution)/shard_map/all_to_all | solution.py:99
  289.0 1.4 gather_fusion.4
  290.3 0.7 convert_reduce_fusion.1
  291.8 2.5 gather_fusion.5
  294.5 51.9 %all_to_all.31 = bf16[8,64,2048]{2,1,0:T(8,128)(2,1)S(1)} all-to-all(bf16[8,64,2048]{2,1,0:T(8,128)(2,1)S(1)} %broadcast_select_fusion), channel_id=1, replica_groups=mesh['dp'=4,'expert'=8] {'expert'}, dimensions={0} | all-to-all | bytes 4194304 | tf_op jit(solution)/shard_map/all_to_all | solution.py:108
  346.4 4.9 %fusion.44 = (bf16[8,2,32]{2,0,1:T(8,128)(2,1)S(1)}, f32[2,8,32,768]{3,2,1,0:T(8,128)S(1)}) fusion(f32[2,8,2,32,768]{4,3,1,2,0:T(8,128)S(1)} %copy-done.8, f32[2,8,2,32,768]{4,3,1,0,2:T(8,128)S(1)} %copy-done.6, bf16[2,768,2048]{2,1,0:T(8,128)(2,1)} %all-gather.8.cloned.1.call-done, bf16[8,2,32,2048]{3,2,1,0:T(8,128)(2,1)S(1)} %bitcast.170), kind=kOutput, calls=%fused_computation.51 | convolution fusion | flops 1613364736 | bytes 13108224 | tf_op jit(solution)/shard_map/slkd,lfd->slkf/dot_general | solution.py:110
  352.0 3.3 all-to-all-start.5
  355.3 5.5 %fusion = f32[2,8,32,2048]{3,2,1,0:T(8,128)S(1)} fusion(bf16[2,2048,768]{2,1,0:T(8,128)(2,1)} %all-gather.6.cloned.1.call-done, f32[2,8,32,768]{3,2,1,0:T(8,128)S(1)} %get-tuple-element.21, f32[8,2,32]{2,0,1:T(8,128)S(1)} %copy.131, f32[2,8,2,32,768]{4,3,1,0,2:T(8,128)} %fusion.27), kind=kOutput, calls=%fused_computation.9 | convolution fusion | flops 1613365248 | bytes 13633536 | tf_op jit(solution)/shard_map/slkf,ldf->slkd/dot_general | solution.py:120
  360.8 5.1 %fusion.19 = bf16[8,2,32,2048]{3,2,0,1:T(8,128)(2,1)S(1)} fusion(f32[2,8,32,2048]{3,2,1,0:T(8,128)S(1)} %fusion, bf16[2,2048,768]{2,1,0:T(8,128)(2,1)} %all-gather.4.cloned.1.call-done, f32[2,8,32,768]{3,2,1,0:T(8,128)S(1)} %get-tuple-element.21, f32[2,8,2,32,768]{4,3,1,2,0:T(8,128)S(1)} %copy-done.9, f32[8,2,32]{2,0,1:T(8,128)S(1)} %copy.131, ...), kind=kOutput, calls=%fused_computation.26 | convolution fusion | flops 1617035264 | bytes 17309696 | tf_op jit(solution)/shard_map/slkf,ldf->slkd/dot_general | solution.py:117
  365.9 1.6 copy.134
  367.5 5.0 %all-to-all-start.4 = ((bf16[8,64,2048]{2,1,0:T(8,128)(2,1)}), bf16[8,64,2048]{2,1,0:T(8,128)(2,1)S(1)}, u32[]{:S(2)}, u32[]{:S(2)}) async-start(bf16[8,64,2048]{2,1,0:T(8,128)(2,1)} %bitcast.168), calls=%async_computation.4 | async-start | bytes 4194304 | tf_op jit(solution)/shard_map/all_to_all | solution.py:128
  372.7 1.9 gather_fusion.7
  374.8 46.8 %all-to-all-done.4 = bf16[8,64,2048]{2,1,0:T(8,128)(2,1)S(1)} async-done(((bf16[8,64,2048]{2,1,0:T(8,128)(2,1)}), bf16[8,64,2048]{2,1,0:T(8,128)(2,1)S(1)}, u32[]{:S(2)}, u32[]{:S(2)}) %all-to-all-start.4) | async-done | bytes 2097184 | tf_op jit(solution)/shard_map/all_to_all | solution.py:128
  421.6 1.4 gather_fusion.6
  424.1 0.8 fusion.57
  (83 shorter events, 8.5 us)
Async XLA Ops:
  7.2 4.7 %copy-start = (bf16[2048,16]{0,1:T(8,128)(2,1)S(1)}, bf16[2048,16]{0,1:T(8,128)(2,1)}, u32[]{:S(2)}) copy-start(bf16[2048,16]{0,1:T(8,128)(2,1)} %param.11) | copy-start | bytes 196612
  7.2 1.5 copy-start.4
  7.2 4.3 copy-start.1
  7.2 4.3 copy-start.3
  7.2 4.5 %copy-start.5 = (f32[2048]{0:T(1024)S(1)}, f32[2048]{0:T(1024)}, u32[]{:S(2)}) copy-start(f32[2048]{0:T(1024)} %param.10) | copy-start | bytes 24580
  7.2 130.9 %all-gather.4.cloned.1.call-start = ((), (), s32[]{:S(2)}) async-start(), calls=%async_computation.6 | async-start | bytes 7864320 | tf_op jit(solution)/shard_map/all_gather | solution.py:75
  8.0 146.9 %all-gather.6.cloned.1.call-start = ((), (), s32[]{:S(2)}) async-start(), calls=%async_computation.7 | async-start | bytes 7864320 | tf_op jit(solution)/shard_map/all_gather | solution.py:76
  22.4 16.5 %all-to-all-start = ((bf16[2,8,64]{2,0,1:T(2,128)(2,1)}), bf16[2,8,64]{2,0,1:T(2,128)(2,1)S(1)}, u32[]{:S(2)}, u32[]{:S(2)}) async-start(bf16[2,8,64]{2,0,1:T(2,128)(2,1)} %copy.122), calls=%async_computation | async-start | bytes 8192 | tf_op jit(solution)/shard_map/all_to_all | solution.py:68
  38.9 99.2 %all-to-all-start.1 = ((bf16[2,8,64,2048]{3,2,0,1:T(8,128)(2,1)}), bf16[2,8,64,2048]{3,2,0,1:T(8,128)(2,1)}, u32[]{:S(2)}, u32[]{:S(2)}) async-start(bf16[2,8,64,2048]{3,2,0,1:T(8,128)(2,1)} %pad_maximum_fusion), calls=%async_computation.1 | async-start | bytes 8388608 | tf_op jit(solution)/shard_map/all_to_all | solution.py:67
  44.0 182.7 %all-gather.8.cloned.1.call-start = ((), (), s32[]{:S(2)}) async-start(), calls=%async_computation.8 | async-start | bytes 7864320 | tf_op jit(solution)/shard_map/all_gather | solution.py:77
  235.3 53.6 %all-to-all-start.2 = ((bf16[8,64,2048]{2,1,0:T(8,128)(2,1)}), bf16[8,64,2048]{2,1,0:T(8,128)(2,1)S(1)}, u32[]{:S(2)}, u32[]{:S(2)}) async-start(bf16[8,64,2048]{2,1,0:T(8,128)(2,1)} %bitcast.169), calls=%async_computation.2 | async-start | bytes 4194304 | tf_op jit(solution)/shard_map/all_to_all | solution.py:99
  291.1 0.7 copy-start.2
  294.3 52.1 %copy-start.8 = (f32[2,8,2,32,768]{4,3,1,2,0:T(8,128)S(1)}, f32[2,8,2,32,768]{4,3,1,2,0:T(8,128)}, u32[]{:S(2)}) copy-start(f32[2,8,2,32,768]{4,3,1,2,0:T(8,128)} %fusion.32) | copy-start | bytes 9437188
  294.5 51.9 %copy-start.6 = (f32[2,8,2,32,768]{4,3,1,0,2:T(8,128)S(1)}, f32[2,8,2,32,768]{4,3,1,0,2:T(8,128)}, u32[]{:S(2)}) copy-start(f32[2,8,2,32,768]{4,3,1,0,2:T(8,128)} %fusion.27) | copy-start | bytes 9437188
  352.0 15.6 %all-to-all-start.5 = ((bf16[8,1,64]{2,1,0:T(2,128)(2,1)}), bf16[8,1,64]{2,1,0:T(2,128)(2,1)S(1)}, u32[]{:S(2)}, u32[]{:S(2)}) async-start(bf16[8,1,64]{2,1,0:T(2,128)(2,1)} %convert_element_type.118), calls=%async_computation.5 | async-start | bytes 8192 | tf_op jit(solution)/shard_map/all_to_all | solution.py:129
  355.3 5.5 %copy-start.7 = (f32[2,8,2,32,768]{4,3,1,0,2:T(8,128)S(1)}, f32[2,8,2,32,768]{4,3,1,0,2:T(8,128)}, u32[]{:S(2)}) copy-start(f32[2,8,2,32,768]{4,3,1,0,2:T(8,128)} %fusion.27) | copy-start | bytes 9437188
  355.3 5.5 %copy-start.9 = (f32[2,8,2,32,768]{4,3,1,2,0:T(8,128)S(1)}, f32[2,8,2,32,768]{4,3,1,2,0:T(8,128)}, u32[]{:S(2)}) copy-start(f32[2,8,2,32,768]{4,3,1,2,0:T(8,128)} %fusion.32) | copy-start | bytes 9437188
  367.5 54.1 %all-to-all-start.4 = ((bf16[8,64,2048]{2,1,0:T(8,128)(2,1)}), bf16[8,64,2048]{2,1,0:T(8,128)(2,1)S(1)}, u32[]{:S(2)}, u32[]{:S(2)}) async-start(bf16[8,64,2048]{2,1,0:T(8,128)(2,1)} %bitcast.168), calls=%async_computation.4 | async-start | bytes 4194304 | tf_op jit(solution)/shard_map/all_to_all | solution.py:128
Sparse Core Ops, SparseCore 0:
  9.9 72.8 all-gather.3
  84.6 70.1 all-gather.5
  156.7 70.0 all-gather.7
where the time goes:
time: 432 us; the launch traced here: 431 us
  waiting for transfers between devices  261 us (60%)
  blocking collectives  51.9 us (12%)
  matrix products  41.7 us (10%)
  local copies, waits for them, and re-layouts  29.8 us (7%)
  starting transfers between devices  24.6 us (6%)
  between operations  14.1 us (3%)
  other arithmetic  8.12 us (2%)
    all_to_all x1, waiting for transfers between devices, on_device(): lax.all_to_all(send_rows, 'expert', split_axis=1, concat_axis=1, tiled=True)  93.2 us
    all_gather x1, waiting for transfers between devices, on_device(): lax.all_gather(w_down, 'dp', axis=2, tiled=True)  62.7 us
    all_to_all x1, blocking collectives, on_device(): lax.all_to_all(send_cot, 'expert', split_axis=0, concat_axis=0, tiled=True)  51.9 us
    all_to_all x1, waiting for transfers between devices, on_device(): lax.all_to_all(pair_send, 'expert', split_axis=0, concat_axis=0, tiled=True)  49.1 us
    all_to_all x1, waiting for transfers between devices, on_device(): lax.all_to_all(grad_send, 'expert', split_axis=0, concat_axis=0, tiled=True)  46.8 us
    dot_general x1, matrix products, on_device(): jnp.einsum('tslkd,ldf->tslkf', slot_rows, up_full, preferred_element_type...  9.17 us
    dot_general x1, matrix products, on_device(): jnp.einsum('tslkd,ldf->tslkf', slot_rows, gate_full, preferred_element_ty...  9.1 us
  transfers between devices with their start and end apart: 8, of which 5 were waited for; matrix products, arithmetic and copies ran while one was open for 13% of the time, Pallas kernels for 0%

commit v1 on v0

--- a/solution.py
+++ b/solution.py
@@ -1,6 +1,8 @@
 import jax
 import jax.numpy as jnp
 from jax import lax
+from jax.experimental import pallas as pl
+from jax.experimental.pallas import tpu as pltpu
 from jax.sharding import PartitionSpec as P
 
 eps_value = 1e-06
@@ -37,13 +39,14 @@
     gate_tan_b = gate_tan.astype(jnp.bfloat16)
     pair_count = tok_rows * topk
     flat_ids = routes.reshape(-1)
-    onehot = (flat_ids[:, None] == jnp.arange(experts_all, dtype=jnp.int32)[None, :]).astype(
-        jnp.int32
-    )
-    slot_rank = jnp.sum(onehot * jnp.cumsum(onehot, axis=0), axis=1) - 1
+    order = jnp.arange(pair_count, dtype=jnp.int32)
+    earlier = (flat_ids[None, :] == flat_ids[:, None]) & (order[None, :] < order[:, None])
+    slot_rank = jnp.sum(earlier.astype(jnp.int32), axis=1)
     slot_of_pair = flat_ids * capacity + slot_rank
-    slot_table = jnp.full((experts_all * capacity,), -1, jnp.int32)
-    slot_table = slot_table.at[slot_of_pair].set(jnp.arange(pair_count, dtype=jnp.int32))
+    slot_hits = slot_of_pair[None, :] == jnp.arange(experts_all * capacity, dtype=jnp.int32)[:, None]
+    slot_table = jnp.max(
+        jnp.where(slot_hits, jnp.arange(pair_count, dtype=jnp.int32)[None, :], -1), axis=1
+    )
     slot_valid = slot_table >= 0
     safe_pair = jnp.maximum(slot_table, 0)
     tok_idx = safe_pair // topk
@@ -147,6 +150,315 @@
     return (tangent_image, gram_image)
 
 
+MESH = pl.DeviceIdType.MESH
+SHIFTS = [(dx, dz) for dx in range(2) for dz in range(4) if dx or dz]
+
+
+def nt_dot(left, right):
+    return lax.dot_general(
+        left, right, (((1,), (1,)), ((), ())), preferred_element_type=jnp.float32
+    )
+
+
+def block_kernel(
+    tok_ref, tan_ref, gain_ref, router_ref, routes_ref, wg_ref, wu_ref, wd_ref,
+    image_ref, gram_ref,
+    wgu, wd, rows, pre, mix, part, cross, summed, landed, image_rows,
+    grads, part2, cross2, summed2, landed2, prob_keep, inv_keep,
+    w_send, w_recv, w_own, a_send, a_recv, r_send, r_recv, c_send, c_recv,
+):
+    f32, bf = jnp.float32, jnp.bfloat16
+    n_tok, width = tok_ref.shape
+    slab, hid = wg_ref.shape[1], wg_ref.shape[2]
+    half = hid // 2
+    dp, ex = lax.axis_index("dp"), lax.axis_index("expert")
+    y, x = dp // 2, dp % 2
+    z, core = ex // 2, ex % 2
+    other = 1 - core
+    slot = x * 4 + z
+    slot_rows = pl.ds(pl.multiple_of(slot * n_tok, n_tok), n_tok)
+    mate = (dp, z * 2 + other)
+
+    def same_core(dx, dz):
+        return (y * 2 + (x + dx) % 2, (z + dz) % 4 * 2 + core)
+
+    def same_slot(dx, dz):
+        return (x + dx) % 2 * 4 + (z + dz) % 4
+
+    plane = [(0, 1), (1, 0), (1, 1)]
+
+    def in_plane(my, mx):
+        return ((y + my) % 2 * 2 + (x + mx) % 2, ex)
+
+    barrier = pltpu.get_barrier_semaphore()
+    friends = [same_core(dx, dz) for dx, dz in SHIFTS] + [mate, in_plane(1, 0), in_plane(1, 1)]
+    for friend in friends:
+        pl.semaphore_signal(barrier, inc=1, device_id=friend, device_id_type=MESH)
+    pl.semaphore_wait(barrier, len(friends))
+
+    slab_rows = pl.ds(pl.multiple_of(dp * slab, slab), slab)
+
+    def weight_ends(kind, l, to_x):
+        cols = pl.ds(pl.multiple_of(to_x * half, half), half)
+        if kind == 0:
+            return wg_ref.at[l, :, cols], wgu.at[l, slab_rows, pl.ds(0, half)]
+        if kind == 1:
+            return wu_ref.at[l, :, cols], wgu.at[l, slab_rows, pl.ds(half, half)]
+        return wd_ref.at[l, cols, :], wd.at[pl.ds(l * half, half), slab_rows]
+
+    moving = {}
+
+    def start_weights(kind, l):
+        copies = []
+        for p, (my, mx) in enumerate(plane):
+            src, dst = weight_ends(kind, l, (x + mx) % 2)
+            copies.append(
+                pltpu.make_async_remote_copy(
+                    src_ref=src, dst_ref=dst,
+                    send_sem=w_send.at[kind, l, p], recv_sem=w_recv.at[kind, l, p],
+                    device_id=in_plane(my, mx), device_id_type=MESH,
+                )
+            )
+        for copy in copies:
+            copy.start()
+        src, dst = weight_ends(kind, l, x)
+        own = pltpu.make_async_copy(src, dst, w_own.at[kind, l])
+        own.start()
+        moving[kind, l] = (copies, own)
+
+    def need_weights(kind, l):
+        copies, own = moving[kind, l]
+        own.wait()
+        for copy in copies:
+            copy.wait_recv()
+
+    def spread(buf, turn):
+        copies = []
+        for i, (dx, dz) in enumerate(SHIFTS):
+            copies.append(
+                pltpu.make_async_remote_copy(
+                    src_ref=buf.at[core, slot_rows], dst_ref=buf.at[core, slot_rows],
+                    send_sem=a_send.at[turn, i], recv_sem=a_recv.at[turn, i],
+                    device_id=same_core(dx, dz), device_id_type=MESH,
+                )
+            )
+        for copy in copies:
+            copy.start()
+        return copies
+
+    def to_mate(src, dst, turn):
+        copy = pltpu.make_async_remote_copy(
+            src_ref=src, dst_ref=dst, send_sem=c_send.at[turn], recv_sem=c_recv.at[turn],
+            device_id=mate, device_id_type=MESH,
+        )
+        copy.start()
+        return copy
+
+    def send_home(own_part, from_mate, out, land, turn):
+        out[...] = (own_part.astype(f32) + from_mate.astype(f32)).astype(bf)
+        copies = []
+        for i, (dx, dz) in enumerate(SHIFTS):
+            there = pl.ds(pl.multiple_of(same_slot(dx, dz) * n_tok, n_tok), n_tok)
+            copies.append(
+                pltpu.make_async_remote_copy(
+                    src_ref=out.at[there], dst_ref=land.at[slot],
+                    send_sem=r_send.at[turn, i], recv_sem=r_recv.at[turn, i],
+                    device_id=same_core(dx, dz), device_id_type=MESH,
+                )
+            )
+        for copy in copies:
+            copy.start()
+        land[slot] = out[slot_rows, :]
+        for copy in copies:
+            copy.wait_recv()
+        total = land[0].astype(f32)
+        for i in range(1, 8):
+            total = total + land[i].astype(f32)
+        return total, copies
+
+    start_weights(0, 0)
+
+    xfull = tok_ref[...].astype(f32)
+    vfull = tan_ref[...].astype(f32)
+    gain = gain_ref[...]
+    inv_rms = lax.rsqrt(jnp.mean(xfull * xfull, axis=1, keepdims=True) + eps_value)
+    normed = (gain * xfull * inv_rms).astype(bf)
+    cross_term = jnp.mean(xfull * vfull, axis=1, keepdims=True)
+    inv_cube = inv_rms * inv_rms * inv_rms
+    normed_tan = (gain * (vfull * inv_rms - xfull * inv_cube * cross_term)).astype(bf)
+    rows[core, slot_rows, 0:width] = normed
+    rows[core, slot_rows, width : 2 * width] = normed_tan
+    logits = jnp.dot(normed, router_ref[...], preferred_element_type=f32)
+    logit_tan = jnp.dot(normed_tan, router_ref[...], preferred_element_type=f32)
+    lanes = lax.broadcasted_iota(jnp.int32, (n_tok, 128), 1)
+    chosen = jnp.zeros((n_tok, 128), f32)
+    for k in range(routes_ref.shape[1]):
+        chosen = chosen + jnp.where(lanes == routes_ref[:, k : k + 1], 1.0, 0.0)
+    exp_sel = jnp.where(chosen > 0.5, jnp.exp(logits), 0.0)
+    gate_prob = exp_sel / jnp.sum(exp_sel, axis=1, keepdims=True)
+    gate_tan = gate_prob * (
+        logit_tan - jnp.sum(gate_prob * logit_tan, axis=1, keepdims=True)
+    )
+    rows[core, slot_rows, 2 * width : 2 * width + 128] = gate_prob.astype(bf)
+    rows[core, slot_rows, 2 * width + 128 : 2 * width + 256] = gate_tan.astype(bf)
+    prob_keep[...] = gate_prob
+    inv_keep[...] = jnp.broadcast_to(inv_rms, (n_tok, 128))
+
+    sent = spread(rows, 0)
+    pending = list(sent)
+    start_weights(1, 0)
+    start_weights(0, 1)
+    start_weights(1, 1)
+    start_weights(2, 0)
+    start_weights(2, 1)
+    for copy in sent:
+        copy.wait_recv()
+    copy = to_mate(rows.at[core], rows.at[core], 0)
+    pending.append(copy)
+    copy.wait_recv()
+
+    n_rows = rows.shape[1]
+    wide_lanes = lax.broadcasted_iota(jnp.int32, (n_rows, 128), 1)
+
+    def gate_of(part_no, l, offset):
+        table = rows[part_no, :, 2 * width + offset : 2 * width + offset + 128].astype(f32)
+        return jnp.sum(jnp.where(wide_lanes == ex * 2 + l, table, 0.0), axis=1, keepdims=True)
+
+    for l in range(2):
+        need_weights(0, l)
+        need_weights(1, l)
+
+        @pl.loop(0, 2)
+        def _(h):
+            pre[l, h] = jnp.dot(rows[h, :, 0:width], wgu[l], preferred_element_type=f32)
+            dots = jnp.dot(rows[h, :, width : 2 * width], wgu[l], preferred_element_type=f32)
+            pre_gate, pre_up = pre[l, h, :, 0:half], pre[l, h, :, half:hid]
+            gate_dot, up_dot = dots[:, 0:half], dots[:, half:hid]
+            sig = jax.nn.sigmoid(pre_gate)
+            silu = pre_gate * sig
+            slope = sig * (1.0 + pre_gate * (1.0 - sig))
+            hidden_tan = slope * gate_dot * pre_up + silu * up_dot
+            mixed = gate_of(h, l, 128) * (silu * pre_up) + gate_of(h, l, 0) * hidden_tan
+            mix[h, :, l * half : (l + 1) * half] = mixed.astype(bf)
+
+    need_weights(2, 0)
+    need_weights(2, 1)
+
+    def down(part_no):
+        part[part_no] = jnp.dot(mix[part_no], wd[...], preferred_element_type=f32).astype(bf)
+
+    down(other)
+    copy = to_mate(part.at[other], cross, 1)
+    pending.append(copy)
+    down(core)
+    copy.wait_recv()
+    image, sent = send_home(part[core], cross[...], summed, landed, 0)
+    pending.extend(sent)
+    image_ref[...] = image
+    image_rows[core, slot_rows, :] = image.astype(bf)
+    sent = spread(image_rows, 1)
+    pending.extend(sent)
+    for copy in sent:
+        copy.wait_recv()
+    copy = to_mate(image_rows.at[core], image_rows.at[core], 2)
+    pending.append(copy)
+
+    def backward(part_no):
+        back = nt_dot(image_rows[part_no], wd[...])
+        cots = jnp.zeros((n_rows, 128), f32)
+        for l in range(2):
+            back_hidden = back[:, l * half : (l + 1) * half]
+            pre_gate, pre_up = pre[l, part_no, :, 0:half], pre[l, part_no, :, half:hid]
+            sig = jax.nn.sigmoid(pre_gate)
+            silu = pre_gate * sig
+            slope = sig * (1.0 + pre_gate * (1.0 - sig))
+            cot = jnp.sum(back_hidden * (silu * pre_up), axis=1, keepdims=True)
+            cots = cots + jnp.where(wide_lanes == ex * 2 + l, cot, 0.0)
+            scaled = gate_of(part_no, l, 0) * back_hidden
+            grads[l, :, 0:half] = (scaled * pre_up * slope).astype(bf)
+            grads[l, :, half:hid] = (scaled * silu).astype(bf)
+        total = nt_dot(grads[0], wgu[0]) + nt_dot(grads[1], wgu[1])
+        part2[part_no, :, 0:width] = total.astype(bf)
+        part2[part_no, :, width : width + 128] = cots.astype(bf)
+
+    backward(core)
+    copy.wait_recv()
+    backward(other)
+    copy = to_mate(part2.at[other], cross2, 3)
+    pending.append(copy)
+    copy.wait_recv()
+    total, sent = send_home(part2[core], cross2[...], summed2, landed2, 1)
+    pending.extend(sent)
+
+    expert_grad = total[:, 0:width]
+    cot = total[:, width : width + 128]
+    prob = prob_keep[...]
+    column_grad = prob * (cot - jnp.sum(prob * cot, axis=1, keepdims=True))
+    high = column_grad.astype(bf)
+    rest = column_grad - high.astype(f32)
+    middle = rest.astype(bf)
+    low = (rest - middle.astype(f32)).astype(bf)
+    router = router_ref[...]
+    router_grad = nt_dot(high, router) + (nt_dot(middle, router) + nt_dot(low, router))
+    xfull = tok_ref[...].astype(f32)
+    inv_rms = inv_keep[:, 0:1]
+    pulled = gain_ref[...] * (expert_grad + router_grad)
+    gram_ref[...] = inv_rms * pulled - xfull * (inv_rms * inv_rms * inv_rms) * jnp.mean(
+        pulled * xfull, axis=1, keepdims=True
+    )
+    for copy in pending:
+        copy.wait_send()
+    for copies, _ in moving.values():
+        for copy in copies:
+            copy.wait_send()
+
+
+def on_device_dense(tokens, tangent, norm_gain, router, w_gate, w_up, w_down, routes):
+    n_tok, width = tokens.shape
+    hid = w_gate.shape[2]
+    n_rows = 8 * n_tok
+    bf, f32 = jnp.bfloat16, jnp.float32
+    wide_router = jnp.pad(router, ((0, 0), (0, 128 - router.shape[1])))
+    vm = pl.BlockSpec(memory_space=pltpu.VMEM)
+    hbm = pl.BlockSpec(memory_space=pl.ANY)
+    out = jax.ShapeDtypeStruct((n_tok, width), f32)
+    dma = pltpu.SemaphoreType.DMA
+    image, gram = pl.pallas_call(
+        block_kernel,
+        out_shape=(out, out),
+        in_specs=[vm] * 5 + [hbm] * 3,
+        out_specs=(vm, vm),
+        scratch_shapes=[
+            pltpu.VMEM((2, width, hid), bf),
+            pltpu.VMEM((hid, width), bf),
+            pltpu.VMEM((2, n_rows, 2 * width + 256), bf),
+            pltpu.VMEM((2, 2, n_rows, hid), f32),
+            pltpu.VMEM((2, n_rows, hid), bf),
+            pltpu.VMEM((2, n_rows, width), bf),
+            pltpu.VMEM((n_rows, width), bf),
+            pltpu.VMEM((n_rows, width), bf),
+            pltpu.VMEM((8, n_tok, width), bf),
+            pltpu.VMEM((2, n_rows, width), bf),
+            pltpu.VMEM((2, n_rows, hid), bf),
+            pltpu.VMEM((2, n_rows, width + 128), bf),
+            pltpu.VMEM((n_rows, width + 128), bf),
+            pltpu.VMEM((n_rows, width + 128), bf),
+            pltpu.VMEM((8, n_tok, width + 128), bf),
+            pltpu.VMEM((n_tok, 128), f32),
+            pltpu.VMEM((n_tok, 128), f32),
+            dma((3, 2, 3)), dma((3, 2, 3)), dma((3, 2)),
+            dma((2, 7)), dma((2, 7)), dma((2, 7)), dma((2, 7)), dma((4,)), dma((4,)),
+        ],
+        compiler_params=pltpu.CompilerParams(
+            collective_id=0, has_side_effects=True, vmem_limit_bytes=56 * 2**20
+        ),
+        cost_estimate=pl.CostEstimate(
+            flops=2 * 16 * n_rows * width * hid, bytes_accessed=2**24, transcendentals=2**20
+        ),
+    )(tokens, tangent, norm_gain.reshape(1, width), wide_router, routes, w_gate, w_up, w_down)
+    return image, gram
+
+
 def solution(mesh):
     in_specs = (
         P(("dp", "expert"), None),
@@ -159,6 +471,9 @@
         P(("dp", "expert"), None),
     )
     out_specs = (P(("dp", "expert"), None), P(("dp", "expert"), None))
+    body = on_device
+    if mesh.shape["dp"] == 4 and mesh.shape["expert"] == 8:
+        body = on_device_dense
     return jax.shard_map(
-        on_device, mesh=mesh, in_specs=in_specs, out_specs=out_specs, check_vma=False
-    )
+        body, mesh=mesh, in_specs=in_specs, out_specs=out_specs, check_vma=False
+    )

time: 432 us -> 230 us (0.53)
  waiting for transfers between devices: 261 us -> 0 us
  Pallas kernels: 0 us -> 221 us
  blocking collectives: 51.9 us -> 0 us
  matrix products: 41.7 us -> 0 us
  starting transfers between devices: 24.6 us -> 0 us
  local copies, waits for them, and re-layouts: 29.8 us -> 6.71 us
  between operations: 14.1 us -> 0.65 us
  other arithmetic: 8.12 us -> 0 us
    pallas_call x0 -> x1, Pallas kernels: none -> 221 us  [on_device_dense(): pl.pallas_call(block_kernel, out_shape=(out, out), in_specs=[vm] * 5 + [h...]
    all_to_all x5 -> x0, waiting for transfers between devices: 189 us -> none  [the longest x1 93.2 us: on_device(): lax.all_to_all(send_rows, 'expert', split_axis=1, concat_axis=1, tiled=True)]
    all_gather x3 -> x0, waiting for transfers between devices: 70.3 us -> none  [the longest x1 62.7 us: on_device(): lax.all_gather(w_down, 'dp', axis=2, tiled=True)]
    all_to_all x1 -> x0, blocking collectives: 51.9 us -> none  [on_device(): lax.all_to_all(send_cot, 'expert', split_axis=0, concat_axis=0, tiled=True)]
    dot_general x9 -> x0, matrix products: 41.7 us -> none  [the longest x1 9.17 us: on_device(): jnp.einsum('tslkd,ldf->tslkf', slot_rows, up_full, preferred_element_type...]
    all_to_all x5 -> x0, starting transfers between devices: 24.3 us -> none  [the longest x1 6.33 us: on_device(): lax.all_to_all(send_gates, 'expert', split_axis=1, concat_axis=1, tiled=T...]
    gather x8 -> x0, local copies, waits for them, and re-layouts: 22.1 us -> none  [the longest x1 4.61 us: on_device(): gate_tan_b[tok_idx, which_k]]
    unnamed x21 -> x4, local copies, waits for them, and re-layouts: 0.82 us -> 5.82 us
  transfers between devices with their start and end apart: 8 -> 0, of which waited for: 5 -> 0; matrix products, arithmetic and copies ran while one was open for 13% -> 0% of each run, Pallas kernels for 0% -> 0%
where the time goes in v1:
time: 230 us; the launch traced here: 229 us
  Pallas kernels  221 us (96%)
  local copies, waits for them, and re-layouts  6.71 us (3%)
    pallas_call x1, Pallas kernels, on_device_dense(): pl.pallas_call(block_kernel, out_shape=(out, out), in_specs=[vm] * 5 + [h...  221 us
    unnamed x4, local copies, waits for them, and re-layouts  5.82 us

profile of v1, /device:TPU:0, one launch (start us, length us, event | category | flops | bytes accessed | tf_op | source)
XLA Modules:
  0.0 228.6 jit_solution(12888313959590938162)
XLA Ops:
  0.6 1.4 copy.11.routes_ref
  2.0 1.1 copy.10
  3.1 0.9 pad.4.router_ref
  4.0 221.3 %shard_map.95 = (f32[32,2048]{1,0:T(8,128)}, f32[32,2048]{1,0:T(8,128)}) custom-call(bf16[32,2048]{1,0:T(8,128)(2,1)} %tok_ref.1, bf16[32,2048]{1,0:T(8,128)(2,1)} %tan_ref.1, f32[1,2048]{1,0:T(1,128)} %bitcast.1, bf16[2048,128]{1,0:T(8,128)(2,1)} %pad.4.router_ref, s32[32,8]{1,0:T(8,128)} %copy.11.routes_ref, bf16[2,512,768]{2,1,0:T(8,128)(2,1)} %wg_ref.1, ...), custom_call_target="tpu_custom_call" | custom-call | flops 12884901888 | bytes 16777216 | tf_op jit(solution)/shard_map/pallas_call | solution.py:426
  225.3 1.7 copy.14
  227.0 1.7 copy.15

commit v2 on v1

--- a/solution.py
+++ b/solution.py
@@ -151,7 +151,6 @@
 
 
 MESH = pl.DeviceIdType.MESH
-SHIFTS = [(dx, dz) for dx in range(2) for dz in range(4) if dx or dz]
 
 
 def nt_dot(left, right):
@@ -163,118 +162,166 @@
 def block_kernel(
     tok_ref, tan_ref, gain_ref, router_ref, routes_ref, wg_ref, wu_ref, wd_ref,
     image_ref, gram_ref,
-    wgu, wd, rows, pre, mix, part, cross, summed, landed, image_rows,
-    grads, part2, cross2, summed2, landed2, prob_keep, inv_keep,
+    wgu, wd, rows, pre, mix, part, cross, summed, far, landed, image_rows,
+    grads, part2, cross2, summed2, far2, landed2, prob_keep, inv_keep,
     w_send, w_recv, w_own, a_send, a_recv, r_send, r_recv, c_send, c_recv,
 ):
     f32, bf = jnp.float32, jnp.bfloat16
     n_tok, width = tok_ref.shape
     slab, hid = wg_ref.shape[1], wg_ref.shape[2]
     half = hid // 2
+    n_core = 4 * n_tok
     dp, ex = lax.axis_index("dp"), lax.axis_index("expert")
     y, x = dp // 2, dp % 2
     z, core = ex // 2, ex % 2
     other = 1 - core
-    slot = x * 4 + z
-    slot_rows = pl.ds(pl.multiple_of(slot * n_tok, n_tok), n_tok)
+    x_peer = (y * 2 + 1 - x, ex)
+    y_peer = ((1 - y) * 2 + x, ex)
     mate = (dp, z * 2 + other)
-
-    def same_core(dx, dz):
-        return (y * 2 + (x + dx) % 2, (z + dz) % 4 * 2 + core)
-
-    def same_slot(dx, dz):
-        return (x + dx) % 2 * 4 + (z + dz) % 4
-
-    plane = [(0, 1), (1, 0), (1, 1)]
-
-    def in_plane(my, mx):
-        return ((y + my) % 2 * 2 + (x + mx) % 2, ex)
+    z_peers = [(dp, (z + dz) % 4 * 2 + core) for dz in range(1, 4)]
+    core_rows = pl.ds(pl.multiple_of(core * n_core, n_core), n_core)
+    other_rows = pl.ds(pl.multiple_of(other * n_core, n_core), n_core)
+
+    def block_rows(dz):
+        return pl.ds(pl.multiple_of(core * n_core + (z + dz) % 4 * n_tok, n_tok), n_tok)
+
+    def z_rows(dz):
+        return pl.ds(pl.multiple_of((z + dz) % 4 * n_tok, n_tok), n_tok)
+
+    slot_rows = block_rows(0)
 
     barrier = pltpu.get_barrier_semaphore()
-    friends = [same_core(dx, dz) for dx, dz in SHIFTS] + [mate, in_plane(1, 0), in_plane(1, 1)]
+    friends = z_peers + [x_peer, y_peer, mate]
     for friend in friends:
         pl.semaphore_signal(barrier, inc=1, device_id=friend, device_id_type=MESH)
     pl.semaphore_wait(barrier, len(friends))
 
-    slab_rows = pl.ds(pl.multiple_of(dp * slab, slab), slab)
-
-    def weight_ends(kind, l, to_x):
-        cols = pl.ds(pl.multiple_of(to_x * half, half), half)
-        if kind == 0:
-            return wg_ref.at[l, :, cols], wgu.at[l, slab_rows, pl.ds(0, half)]
-        if kind == 1:
-            return wu_ref.at[l, :, cols], wgu.at[l, slab_rows, pl.ds(half, half)]
-        return wd_ref.at[l, cols, :], wd.at[pl.ds(l * half, half), slab_rows]
-
-    moving = {}
+    pending = []
+
+    def push(src, dst, sems, where, device):
+        copy = pltpu.make_async_remote_copy(
+            src_ref=src, dst_ref=dst, send_sem=sems[0].at[where], recv_sem=sems[1].at[where],
+            device_id=device, device_id_type=MESH,
+        )
+        copy.start()
+        pending.append(copy)
+        return copy
+
+    def slab_of(index):
+        return pl.ds(pl.multiple_of(index * slab, slab), slab)
+
+    def weight_dst(kind, l, index):
+        if kind == 2:
+            return wd.at[pl.ds(l * half, half), slab_of(index)]
+        return wgu.at[l, slab_of(index), pl.ds(kind * half, half)]
+
+    def weight_src(kind, l, which):
+        part_of = pl.ds(pl.multiple_of(which * half, half), half)
+        if kind == 2:
+            return wd_ref.at[l, part_of, :]
+        return (wg_ref, wu_ref)[kind].at[l, :, part_of]
+
+    moving, relayed = {}, {}
+    w_sems = (w_send, w_recv)
 
     def start_weights(kind, l):
-        copies = []
-        for p, (my, mx) in enumerate(plane):
-            src, dst = weight_ends(kind, l, (x + mx) % 2)
-            copies.append(
-                pltpu.make_async_remote_copy(
-                    src_ref=src, dst_ref=dst,
-                    send_sem=w_send.at[kind, l, p], recv_sem=w_recv.at[kind, l, p],
-                    device_id=in_plane(my, mx), device_id_type=MESH,
-                )
-            )
-        for copy in copies:
-            copy.start()
-        src, dst = weight_ends(kind, l, x)
-        own = pltpu.make_async_copy(src, dst, w_own.at[kind, l])
+        mine = weight_dst(kind, l, dp)
+        for_x, for_y = (1 - x, x) if l == 0 else (y, 1 - y)
+        own = pltpu.make_async_copy(
+            weight_src(kind, l, x if l == 0 else y), mine, w_own.at[kind, l]
+        )
+        ends = [(for_x, 0, x_peer), (for_y, 1, y_peer)]
+        copies = [
+            push(weight_src(kind, l, which), mine, w_sems, (kind, l, p), peer)
+            for which, p, peer in ends
+        ]
         own.start()
         moving[kind, l] = (copies, own)
+
+    def relay_weights(kind, l):
+        moving[kind, l][0][l].wait_recv()
+        if l == 0:
+            block = weight_dst(kind, l, y * 2 + 1 - x)
+            relayed[kind, l] = push(block, block, w_sems, (kind, l, 2), y_peer)
+        else:
+            block = weight_dst(kind, l, (1 - y) * 2 + x)
+            relayed[kind, l] = push(block, block, w_sems, (kind, l, 2), x_peer)
 
     def need_weights(kind, l):
         copies, own = moving[kind, l]
         own.wait()
+        copies[1 - l].wait_recv()
+        relayed[kind, l].wait_recv()
+
+    a_sems, c_sems, r_sems = (a_send, a_recv), (c_send, c_recv), (r_send, r_recv)
+
+    def gather_start(buf, turn):
+        mine = buf.at[0, slot_rows]
+        along_z = [
+            push(mine, mine, a_sems, (turn, 0, i + 1), peer) for i, peer in enumerate(z_peers)
+        ]
+        sides = [
+            [push(mine, buf.at[1 + s, slot_rows], a_sems, (turn, 1 + s, 0), peer)]
+            for s, peer in enumerate((x_peer, y_peer))
+        ]
+        return along_z, sides
+
+    def gather_finish(buf, turn, started):
+        along_z, sides = started
+        for dz in (3, 1, 2):
+            along_z[dz - 1].wait_recv()
+            got = block_rows(4 - dz)
+            for s, peer in enumerate((x_peer, y_peer)):
+                sides[s].append(
+                    push(buf.at[0, got], buf.at[1 + s, got], a_sems, (turn, 1 + s, dz), peer)
+                )
+        to_mate = [push(buf.at[0, core_rows], buf.at[0, core_rows], c_sems, (turn, 0), mate)]
+        for s in range(2):
+            for copy in sides[s]:
+                copy.wait_recv()
+            block = buf.at[1 + s, core_rows]
+            to_mate.append(push(block, block, c_sems, (turn, 1 + s), mate))
+        return to_mate
+
+    def send_home(compute, parts, crossed, mid, far, land, turn):
+        over, aside = {}, []
+
+        def to_mate(g):
+            over[g] = push(
+                parts.at[g, other_rows], crossed.at[g], c_sems, (2 + turn, g), mate
+            )
+
+        def add_mate(g):
+            over[g].wait_recv()
+            mid[g] = (parts[g, core_rows, :].astype(f32) + crossed[g].astype(f32)).astype(bf)
+
+        def to_side(g, peer):
+            add_mate(g)
+            aside.append(push(mid.at[g], far.at[g - 1], r_sems, (turn, 3 + g), peer))
+
+        compute(1)
+        to_mate(1)
+        compute(2)
+        to_mate(2)
+        to_side(1, x_peer)
+        compute(0)
+        to_mate(0)
+        to_side(2, y_peer)
+        over[0].wait_recv()
+        for copy in aside:
+            copy.wait_recv()
+        own = parts[0, core_rows, :].astype(f32) + crossed[0].astype(f32)
+        mid[0] = (own + (far[0].astype(f32) + far[1].astype(f32))).astype(bf)
+        copies = [
+            push(mid.at[0, z_rows(i + 1)], land.at[z], r_sems, (turn, 1 + i), peer)
+            for i, peer in enumerate(z_peers)
+        ]
+        land[z] = mid[0, z_rows(0), :]
         for copy in copies:
             copy.wait_recv()
-
-    def spread(buf, turn):
-        copies = []
-        for i, (dx, dz) in enumerate(SHIFTS):
-            copies.append(
-                pltpu.make_async_remote_copy(
-                    src_ref=buf.at[core, slot_rows], dst_ref=buf.at[core, slot_rows],
-                    send_sem=a_send.at[turn, i], recv_sem=a_recv.at[turn, i],
-                    device_id=same_core(dx, dz), device_id_type=MESH,
-                )
-            )
-        for copy in copies:
-            copy.start()
-        return copies
-
-    def to_mate(src, dst, turn):
-        copy = pltpu.make_async_remote_copy(
-            src_ref=src, dst_ref=dst, send_sem=c_send.at[turn], recv_sem=c_recv.at[turn],
-            device_id=mate, device_id_type=MESH,
+        return (land[0].astype(f32) + land[1].astype(f32)) + (
+            land[2].astype(f32) + land[3].astype(f32)
         )
-        copy.start()
-        return copy
-
-    def send_home(own_part, from_mate, out, land, turn):
-        out[...] = (own_part.astype(f32) + from_mate.astype(f32)).astype(bf)
-        copies = []
-        for i, (dx, dz) in enumerate(SHIFTS):
-            there = pl.ds(pl.multiple_of(same_slot(dx, dz) * n_tok, n_tok), n_tok)
-            copies.append(
-                pltpu.make_async_remote_copy(
-                    src_ref=out.at[there], dst_ref=land.at[slot],
-                    send_sem=r_send.at[turn, i], recv_sem=r_recv.at[turn, i],
-                    device_id=same_core(dx, dz), device_id_type=MESH,
-                )
-            )
-        for copy in copies:
-            copy.start()
-        land[slot] = out[slot_rows, :]
-        for copy in copies:
-            copy.wait_recv()
-        total = land[0].astype(f32)
-        for i in range(1, 8):
-            total = total + land[i].astype(f32)
-        return total, copies
 
     start_weights(0, 0)
 
@@ -286,8 +333,8 @@
     cross_term = jnp.mean(xfull * vfull, axis=1, keepdims=True)
     inv_cube = inv_rms * inv_rms * inv_rms
     normed_tan = (gain * (vfull * inv_rms - xfull * inv_cube * cross_term)).astype(bf)
-    rows[core, slot_rows, 0:width] = normed
-    rows[core, slot_rows, width : 2 * width] = normed_tan
+    rows[0, slot_rows, 0:width] = normed
+    rows[0, slot_rows, width : 2 * width] = normed_tan
     logits = jnp.dot(normed, router_ref[...], preferred_element_type=f32)
     logit_tan = jnp.dot(normed_tan, router_ref[...], preferred_element_type=f32)
     lanes = lax.broadcasted_iota(jnp.int32, (n_tok, 128), 1)
@@ -299,23 +346,19 @@
     gate_tan = gate_prob * (
         logit_tan - jnp.sum(gate_prob * logit_tan, axis=1, keepdims=True)
     )
-    rows[core, slot_rows, 2 * width : 2 * width + 128] = gate_prob.astype(bf)
-    rows[core, slot_rows, 2 * width + 128 : 2 * width + 256] = gate_tan.astype(bf)
+    rows[0, slot_rows, 2 * width : 2 * width + 128] = gate_prob.astype(bf)
+    rows[0, slot_rows, 2 * width + 128 : 2 * width + 256] = gate_tan.astype(bf)
     prob_keep[...] = gate_prob
     inv_keep[...] = jnp.broadcast_to(inv_rms, (n_tok, 128))
 
-    sent = spread(rows, 0)
-    pending = list(sent)
-    start_weights(1, 0)
-    start_weights(0, 1)
-    start_weights(1, 1)
-    start_weights(2, 0)
-    start_weights(2, 1)
-    for copy in sent:
+    started = gather_start(rows, 0)
+    pieces = [(0, 0), (1, 0), (0, 1), (1, 1), (2, 0), (2, 1)]
+    for kind, l in pieces[1:]:
+        start_weights(kind, l)
+    for copy in gather_finish(rows, 0, started):
         copy.wait_recv()
-    copy = to_mate(rows.at[core], rows.at[core], 0)
-    pending.append(copy)
-    copy.wait_recv()
+    for kind, l in pieces:
+        relay_weights(kind, l)
 
     n_rows = rows.shape[1]
     wide_lanes = lax.broadcasted_iota(jnp.int32, (n_rows, 128), 1)
@@ -330,65 +373,56 @@
 
         @pl.loop(0, 2)
         def _(h):
-            pre[l, h] = jnp.dot(rows[h, :, 0:width], wgu[l], preferred_element_type=f32)
-            dots = jnp.dot(rows[h, :, width : 2 * width], wgu[l], preferred_element_type=f32)
+            g = h * (l + 1)
+            pre[l, h] = jnp.dot(rows[g, :, 0:width], wgu[l], preferred_element_type=f32)
+            dots = jnp.dot(rows[g, :, width : 2 * width], wgu[l], preferred_element_type=f32)
             pre_gate, pre_up = pre[l, h, :, 0:half], pre[l, h, :, half:hid]
             gate_dot, up_dot = dots[:, 0:half], dots[:, half:hid]
             sig = jax.nn.sigmoid(pre_gate)
             silu = pre_gate * sig
             slope = sig * (1.0 + pre_gate * (1.0 - sig))
             hidden_tan = slope * gate_dot * pre_up + silu * up_dot
-            mixed = gate_of(h, l, 128) * (silu * pre_up) + gate_of(h, l, 0) * hidden_tan
-            mix[h, :, l * half : (l + 1) * half] = mixed.astype(bf)
+            mixed = gate_of(g, l, 128) * (silu * pre_up) + gate_of(g, l, 0) * hidden_tan
+            mix[g, :, l * half : (l + 1) * half] = mixed.astype(bf)
 
     need_weights(2, 0)
     need_weights(2, 1)
 
-    def down(part_no):
-        part[part_no] = jnp.dot(mix[part_no], wd[...], preferred_element_type=f32).astype(bf)
-
-    down(other)
-    copy = to_mate(part.at[other], cross, 1)
-    pending.append(copy)
-    down(core)
-    copy.wait_recv()
-    image, sent = send_home(part[core], cross[...], summed, landed, 0)
-    pending.extend(sent)
+    spans = [(0, hid), (0, half), (half, hid)]
+
+    def down(g):
+        lo, hi = spans[g]
+        part[g] = jnp.dot(mix[g, :, lo:hi], wd[lo:hi, :], preferred_element_type=f32).astype(bf)
+
+    image = send_home(down, part, cross, summed, far, landed, 0)
     image_ref[...] = image
-    image_rows[core, slot_rows, :] = image.astype(bf)
-    sent = spread(image_rows, 1)
-    pending.extend(sent)
-    for copy in sent:
+    image_rows[0, slot_rows, :] = image.astype(bf)
+    for copy in gather_finish(image_rows, 1, gather_start(image_rows, 1)):
         copy.wait_recv()
-    copy = to_mate(image_rows.at[core], image_rows.at[core], 2)
-    pending.append(copy)
-
-    def backward(part_no):
-        back = nt_dot(image_rows[part_no], wd[...])
+
+    def backward(g):
+        lo, hi = spans[g]
+        back = nt_dot(image_rows[g], wd[lo:hi, :])
         cots = jnp.zeros((n_rows, 128), f32)
-        for l in range(2):
-            back_hidden = back[:, l * half : (l + 1) * half]
-            pre_gate, pre_up = pre[l, part_no, :, 0:half], pre[l, part_no, :, half:hid]
+        total = None
+        for l in range(lo // half, hi // half):
+            back_hidden = back[:, l * half - lo : (l + 1) * half - lo]
+            h = 1 if g else 0
+            pre_gate, pre_up = pre[l, h, :, 0:half], pre[l, h, :, half:hid]
             sig = jax.nn.sigmoid(pre_gate)
             silu = pre_gate * sig
             slope = sig * (1.0 + pre_gate * (1.0 - sig))
             cot = jnp.sum(back_hidden * (silu * pre_up), axis=1, keepdims=True)
             cots = cots + jnp.where(wide_lanes == ex * 2 + l, cot, 0.0)
-            scaled = gate_of(part_no, l, 0) * back_hidden
+            scaled = gate_of(g, l, 0) * back_hidden
             grads[l, :, 0:half] = (scaled * pre_up * slope).astype(bf)
             grads[l, :, half:hid] = (scaled * silu).astype(bf)
-        total = nt_dot(grads[0], wgu[0]) + nt_dot(grads[1], wgu[1])
-        part2[part_no, :, 0:width] = total.astype(bf)
-        part2[part_no, :, width : width + 128] = cots.astype(bf)
-
-    backward(core)
-    copy.wait_recv()
-    backward(other)
-    copy = to_mate(part2.at[other], cross2, 3)
-    pending.append(copy)
-    copy.wait_recv()
-    total, sent = send_home(part2[core], cross2[...], summed2, landed2, 1)
-    pending.extend(sent)
+            term = nt_dot(grads[l], wgu[l])
+            total = term if total is None else total + term
+        part2[g, :, 0:width] = total.astype(bf)
+        part2[g, :, width : width + 128] = cots.astype(bf)
+
+    total = send_home(backward, part2, cross2, summed2, far2, landed2, 1)
 
     expert_grad = total[:, 0:width]
     cot = total[:, width : width + 128]
@@ -408,9 +442,6 @@
     )
     for copy in pending:
         copy.wait_send()
-    for copies, _ in moving.values():
-        for copy in copies:
-            copy.wait_send()
 
 
 def on_device_dense(tokens, tangent, norm_gain, router, w_gate, w_up, w_down, routes):
@@ -431,26 +462,28 @@
         scratch_shapes=[
             pltpu.VMEM((2, width, hid), bf),
             pltpu.VMEM((hid, width), bf),
-            pltpu.VMEM((2, n_rows, 2 * width + 256), bf),
+            pltpu.VMEM((3, n_rows, 2 * width + 256), bf),
             pltpu.VMEM((2, 2, n_rows, hid), f32),
+            pltpu.VMEM((3, n_rows, hid), bf),
+            pltpu.VMEM((3, n_rows, width), bf),
+            pltpu.VMEM((3, n_rows // 2, width), bf),
+            pltpu.VMEM((3, n_rows // 2, width), bf),
+            pltpu.VMEM((2, n_rows // 2, width), bf),
+            pltpu.VMEM((4, n_tok, width), bf),
+            pltpu.VMEM((3, n_rows, width), bf),
             pltpu.VMEM((2, n_rows, hid), bf),
-            pltpu.VMEM((2, n_rows, width), bf),
-            pltpu.VMEM((n_rows, width), bf),
-            pltpu.VMEM((n_rows, width), bf),
-            pltpu.VMEM((8, n_tok, width), bf),
-            pltpu.VMEM((2, n_rows, width), bf),
-            pltpu.VMEM((2, n_rows, hid), bf),
-            pltpu.VMEM((2, n_rows, width + 128), bf),
-            pltpu.VMEM((n_rows, width + 128), bf),
-            pltpu.VMEM((n_rows, width + 128), bf),
-            pltpu.VMEM((8, n_tok, width + 128), bf),
+            pltpu.VMEM((3, n_rows, width + 128), bf),
+            pltpu.VMEM((3, n_rows // 2, width + 128), bf),
+            pltpu.VMEM((3, n_rows // 2, width + 128), bf),
+            pltpu.VMEM((2, n_rows // 2, width + 128), bf),
+            pltpu.VMEM((4, n_tok, width + 128), bf),
             pltpu.VMEM((n_tok, 128), f32),
             pltpu.VMEM((n_tok, 128), f32),
             dma((3, 2, 3)), dma((3, 2, 3)), dma((3, 2)),
-            dma((2, 7)), dma((2, 7)), dma((2, 7)), dma((2, 7)), dma((4,)), dma((4,)),
+            dma((2, 3, 4)), dma((2, 3, 4)), dma((2, 6)), dma((2, 6)), dma((4, 3)), dma((4, 3)),
         ],
         compiler_params=pltpu.CompilerParams(
-            collective_id=0, has_side_effects=True, vmem_limit_bytes=56 * 2**20
+            collective_id=0, has_side_effects=True, vmem_limit_bytes=60 * 2**20
         ),
         cost_estimate=pl.CostEstimate(
             flops=2 * 16 * n_rows * width * hid, bytes_accessed=2**24, transcendentals=2**20

time: 230 us -> 207 us (0.900)
  Pallas kernels: 221 us -> 197 us
    pallas_call x1, Pallas kernels: 221 us -> 197 us  [on_device_dense(): pl.pallas_call(block_kernel, out_shape=(out, out), in_specs=[vm] * 5 + [h...]
where the time goes in v2:
time: 207 us; the launch traced here: 204 us
  Pallas kernels  197 us (95%)
  local copies, waits for them, and re-layouts  6.71 us (3%)
    pallas_call x1, Pallas kernels, on_device_dense(): pl.pallas_call(block_kernel, out_shape=(out, out), in_specs=[vm] * 5 + [h...  197 us
    unnamed x4, local copies, waits for them, and re-layouts  5.82 us

profile of v2, /device:TPU:0, one launch (start us, length us, event | category | flops | bytes accessed | tf_op | source)
XLA Modules:
  0.0 204.2 jit_solution(6952555776195077234)
XLA Ops:
  0.6 1.4 copy.11.routes_ref
  2.0 1.1 copy.10
  3.1 0.9 pad.4.router_ref
  4.0 196.8 %shard_map.95 = (f32[32,2048]{1,0:T(8,128)}, f32[32,2048]{1,0:T(8,128)}) custom-call(bf16[32,2048]{1,0:T(8,128)(2,1)} %tok_ref.1, bf16[32,2048]{1,0:T(8,128)(2,1)} %tan_ref.1, f32[1,2048]{1,0:T(1,128)} %bitcast.1, bf16[2048,128]{1,0:T(8,128)(2,1)} %pad.4.router_ref, s32[32,8]{1,0:T(8,128)} %copy.11.routes_ref, bf16[2,512,768]{2,1,0:T(8,128)(2,1)} %wg_ref.1, ...), custom_call_target="tpu_custom_call" | custom-call | flops 12884901888 | bytes 16777216 | tf_op jit(solution)/shard_map/pallas_call | solution.py:457
  200.8 1.7 copy.14
  202.5 1.7 copy.15

commit v3 on v2

--- a/solution.py
+++ b/solution.py
@@ -261,30 +261,31 @@
             push(mine, mine, a_sems, (turn, 0, i + 1), peer) for i, peer in enumerate(z_peers)
         ]
         sides = [
-            [push(mine, buf.at[1 + s, slot_rows], a_sems, (turn, 1 + s, 0), peer)]
+            {0: push(mine, buf.at[1 + s, slot_rows], a_sems, (turn, 1 + s, 0), peer)}
             for s, peer in enumerate((x_peer, y_peer))
         ]
-        return along_z, sides
+        return along_z, sides, [push(mine, mine, c_sems, (turn, 0), mate)]
 
     def gather_finish(buf, turn, started):
-        along_z, sides = started
+        along_z, sides, to_mate = started
         for dz in (3, 1, 2):
             along_z[dz - 1].wait_recv()
             got = block_rows(4 - dz)
+            block = buf.at[0, got]
             for s, peer in enumerate((x_peer, y_peer)):
-                sides[s].append(
-                    push(buf.at[0, got], buf.at[1 + s, got], a_sems, (turn, 1 + s, dz), peer)
+                sides[s][dz] = push(
+                    block, buf.at[1 + s, got], a_sems, (turn, 1 + s, dz), peer
                 )
-        to_mate = [push(buf.at[0, core_rows], buf.at[0, core_rows], c_sems, (turn, 0), mate)]
-        for s in range(2):
-            for copy in sides[s]:
-                copy.wait_recv()
-            block = buf.at[1 + s, core_rows]
-            to_mate.append(push(block, block, c_sems, (turn, 1 + s), mate))
+            to_mate.append(push(block, block, c_sems, (turn, dz), mate))
+        for dz in (0, 3, 1, 2):
+            for s in range(2):
+                sides[s][dz].wait_recv()
+                block = buf.at[1 + s, block_rows((4 - dz) % 4)]
+                to_mate.append(push(block, block, c_sems, (turn, 4 + 4 * s + dz), mate))
         return to_mate
 
     def send_home(compute, parts, crossed, mid, far, land, turn):
-        over, aside = {}, []
+        over, aside = {}, {}
 
         def to_mate(g):
             over[g] = push(
@@ -297,31 +298,37 @@
 
         def to_side(g, peer):
             add_mate(g)
-            aside.append(push(mid.at[g], far.at[g - 1], r_sems, (turn, 3 + g), peer))
+            for dz in (2, 1, 3, 0):
+                aside[g, dz] = push(
+                    mid.at[g, z_rows(dz)], far.at[g - 1, z_rows(dz)],
+                    r_sems, (turn, 4 * g + dz), peer,
+                )
 
         compute(1)
         to_mate(1)
         compute(2)
         to_mate(2)
         to_side(1, x_peer)
+        to_side(2, y_peer)
         compute(0)
         to_mate(0)
-        to_side(2, y_peer)
         over[0].wait_recv()
-        for copy in aside:
-            copy.wait_recv()
-        own = parts[0, core_rows, :].astype(f32) + crossed[0].astype(f32)
-        mid[0] = (own + (far[0].astype(f32) + far[1].astype(f32))).astype(bf)
-        copies = [
-            push(mid.at[0, z_rows(i + 1)], land.at[z], r_sems, (turn, 1 + i), peer)
-            for i, peer in enumerate(z_peers)
-        ]
-        land[z] = mid[0, z_rows(0), :]
-        for copy in copies:
-            copy.wait_recv()
-        return (land[0].astype(f32) + land[1].astype(f32)) + (
-            land[2].astype(f32) + land[3].astype(f32)
-        )
+        copies = {}
+        for dz in (2, 1, 3, 0):
+            aside[1, dz].wait_recv()
+            aside[2, dz].wait_recv()
+            at = z_rows(dz)
+            own = parts[0, block_rows(dz), :].astype(f32) + crossed[0, at, :].astype(f32)
+            total = own + (far[0, at, :].astype(f32) + far[1, at, :].astype(f32))
+            if dz:
+                mid[0, at, :] = total.astype(bf)
+                copies[dz] = push(
+                    mid.at[0, at], land.at[z], r_sems, (turn, dz), z_peers[dz - 1]
+                )
+        for dz in (1, 3, 2):
+            copies[dz].wait_recv()
+            total = total + land[(z + 4 - dz) % 4].astype(f32)
+        return total
 
     start_weights(0, 0)
 
@@ -480,7 +487,7 @@
             pltpu.VMEM((n_tok, 128), f32),
             pltpu.VMEM((n_tok, 128), f32),
             dma((3, 2, 3)), dma((3, 2, 3)), dma((3, 2)),
-            dma((2, 3, 4)), dma((2, 3, 4)), dma((2, 6)), dma((2, 6)), dma((4, 3)), dma((4, 3)),
+            dma((2, 3, 4)), dma((2, 3, 4)), dma((2, 12)), dma((2, 12)), dma((4, 12)), dma((4, 12)),
         ],
         compiler_params=pltpu.CompilerParams(
             collective_id=0, has_side_effects=True, vmem_limit_bytes=60 * 2**20

time: 207 us -> 186 us (0.90); the launches traced: 204 us -> 186 us
  Pallas kernels: 197 us -> 179 us
    pallas_call x1, Pallas kernels: 197 us -> 179 us  [on_device_dense(): pl.pallas_call(block_kernel, out_shape=(out, out), in_specs=[vm] * 5 + [h...]
where the time goes in v3:
time: 186 us
  Pallas kernels  179 us (96%)
  local copies, waits for them, and re-layouts  6.71 us (4%)
    pallas_call x1, Pallas kernels, on_device_dense(): pl.pallas_call(block_kernel, out_shape=(out, out), in_specs=[vm] * 5 + [h...  179 us
    unnamed x4, local copies, waits for them, and re-layouts  5.82 us

profile of v3, /device:TPU:0, one launch (start us, length us, event | category | flops | bytes accessed | tf_op | source)
XLA Modules:
  0.0 186.2 jit_solution(4533454249391273098)
XLA Ops:
  0.6 1.4 copy.11.routes_ref
  2.0 1.1 copy.10
  3.1 0.9 pad.4.router_ref
  4.0 178.8 %shard_map.95 = (f32[32,2048]{1,0:T(8,128)}, f32[32,2048]{1,0:T(8,128)}) custom-call(bf16[32,2048]{1,0:T(8,128)(2,1)} %tok_ref.1, bf16[32,2048]{1,0:T(8,128)(2,1)} %tan_ref.1, f32[1,2048]{1,0:T(1,128)} %bitcast.1, bf16[2048,128]{1,0:T(8,128)(2,1)} %pad.4.router_ref, s32[32,8]{1,0:T(8,128)} %copy.11.routes_ref, bf16[2,512,768]{2,1,0:T(8,128)(2,1)} %wg_ref.1, ...), custom_call_target="tpu_custom_call" | custom-call | flops 12884901888 | bytes 16777216 | tf_op jit(solution)/shard_map/pallas_call | solution.py:464
  182.8 1.7 copy.14
  184.5 1.7 copy.15
